TPU v7x, 32 devices: a whole 2x2x4 slice. The times are simulated.
32 devices in a mesh: pass: 8 (over y, x, core), kv: 4 (over z).
Axes of the slice: x: 2, y: 2, z: 4, core: 2. Of those that a mesh axis runs over, the one named last changes fastest.
Arguments:
- queries: bfloat16 [8, 64, 4096], P('pass', None, 'kv'), may hold values from -40 to 40
- suffix_keys: bfloat16 [8, 64, 512], P('pass', None, 'kv'), may hold values from -5 to 5
- suffix_values: bfloat16 [8, 64, 512], P('pass', None, 'kv'), may hold values from -40 to 40
- passage_keys: bfloat16 [32, 1024, 512], P('pass', None, 'kv'), may hold values from -5 to 5
- passage_values: bfloat16 [32, 1024, 512], P('pass', None, 'kv'), may hold values from -40 to 40
- fresh_keys: bfloat16 [8, 8, 128, 512], P('pass', None, None, 'kv'), may hold values from -5 to 5
- fresh_values: bfloat16 [8, 8, 128, 512], P('pass', None, None, 'kv'), may hold values from -40 to 40
- citations: int32 [8, 8], P('pass'), may hold values from 0 to 31, all different within a row; in each aligned block of 8 rows (0 to 7, 8 to 15, ...) at most 4 rows name the same one
- selected: int32 [8, 8, 128], P('pass'), may hold values from 0 to 1023, as said below
Outputs:
- attention: bfloat16 [8, 64, 4096], P('pass', 'kv')
Inputs may be any that keep to these rules, and one draw needn't show every extreme that they name: `citations`: each request cites 8 distinct passages; every passage is cited; no passage is cited by more than 4 requests, a bound that some block reaches. `selected`: each list holds 128 distinct positions of its passage.
All inputs are finite; a program needn't handle non-finite values.
Results may differ from a plain program's by a relative error of at most 0.0053.
Values may be sent and summed in bfloat16 or wider, within the bound.
A program may use at most 128 MiB of HBM per device.

v0:
```python
import math

import jax
import jax.numpy as jnp
from jax import lax
from jax.sharding import PartitionSpec as P

HD = 128
PMOST = 4


very_low = -1e30


def body(
    queries,
    suffix_keys,
    suffix_values,
    passage_keys,
    passage_values,
    fresh_keys,
    fresh_values,
    citations,
    selected,
):
    my_place = lax.axis_index("pass")
    local_requests, suffix_len, row_width = queries.shape
    local_passages, length, kv_width = passage_keys.shape
    kv_heads = kv_width // HD
    group_size = row_width // kv_width
    head_count = kv_heads * group_size
    cite_count = citations.shape[1]
    pick_count = selected.shape[2]
    score_scale = 1.0 / math.sqrt(HD)
    all_cites, all_picks = (
        lax.all_gather(citations, "pass", axis=0, tiled=True),
        lax.all_gather(selected, "pass", axis=0, tiled=True),
    )
    all_queries = lax.all_gather(queries, "pass", axis=0, tiled=True)
    total_requests = all_cites.shape[0]
    own_query = queries.reshape(local_requests, suffix_len, kv_heads, group_size, HD)
    fresh_count = cite_count * pick_count
    fresh_key_rows = fresh_keys.reshape(local_requests, fresh_count, kv_heads, HD)
    fresh_value_rows = fresh_values.reshape(local_requests, fresh_count, kv_heads, HD)
    suffix_key_rows = suffix_keys.reshape(local_requests, suffix_len, kv_heads, HD)
    suffix_value_rows = suffix_values.reshape(local_requests, suffix_len, kv_heads, HD)
    fresh_scores = (
        jnp.einsum(
            "rskgd,rtkd->rskgt", own_query, fresh_key_rows, preferred_element_type=jnp.float32
        )
        * score_scale
    )
    suffix_scores = (
        jnp.einsum(
            "rskgd,rtkd->rskgt", own_query, suffix_key_rows, preferred_element_type=jnp.float32
        )
        * score_scale
    )
    causal = jnp.arange(suffix_len)[None, :] <= jnp.arange(suffix_len)[:, None]
    suffix_scores = jnp.where(causal[None, :, None, None, :], suffix_scores, very_low)
    host_max = jnp.maximum(jnp.max(fresh_scores, axis=-1), jnp.max(suffix_scores, axis=-1))
    fresh_weights = jnp.exp(fresh_scores - host_max[..., None])
    suffix_weights = jnp.exp(suffix_scores - host_max[..., None])
    host_sum = (jnp.sum(fresh_weights, axis=-1) + jnp.sum(suffix_weights, axis=-1)).reshape(
        local_requests, suffix_len, head_count
    )
    host_acc = jnp.einsum(
        "rskgt,rtkd->rskgd",
        fresh_weights.astype(jnp.bfloat16),
        fresh_value_rows,
        preferred_element_type=jnp.float32,
    )
    host_acc = host_acc + jnp.einsum(
        "rskgt,rtkd->rskgd",
        suffix_weights.astype(jnp.bfloat16),
        suffix_value_rows,
        preferred_element_type=jnp.float32,
    )
    host_acc = host_acc.reshape(local_requests, suffix_len, head_count, HD)
    host_max = host_max.reshape(local_requests, suffix_len, head_count)
    local_ids = my_place * local_passages + jnp.arange(local_passages, dtype=jnp.int32)
    hit_table = all_cites[None, :, :] == local_ids[:, None, None]
    cited_here = jnp.any(hit_table, axis=2)
    cite_slot = jnp.sum(
        jnp.where(hit_table, jnp.arange(cite_count, dtype=jnp.int32)[None, None, :], 0), axis=2
    )
    cite_rank = jnp.cumsum(cited_here.astype(jnp.int32), axis=1) - 1
    slot_ids = jnp.arange(PMOST, dtype=jnp.int32)
    slot_hit = cited_here[:, None, :] & (cite_rank[:, None, :] == slot_ids[None, :, None])
    request_ids = jnp.arange(total_requests, dtype=jnp.int32)
    slot_request = jnp.sum(jnp.where(slot_hit, request_ids[None, None, :], 0), axis=2).reshape(-1)
    slot_cite = jnp.sum(jnp.where(slot_hit, cite_slot[:, None, :], 0), axis=2).reshape(-1)
    slot_live = jnp.any(slot_hit, axis=2).reshape(-1)
    positions = jnp.arange(length, dtype=jnp.int32)

    def attend_slot(slot_index, loop_state):
        row_max, row_sum, row_acc = loop_state
        source = slot_index // PMOST
        request = slot_request[slot_index]
        active = slot_live[slot_index]
        query_block = lax.dynamic_index_in_dim(all_queries, request, 0, keepdims=False).reshape(
            suffix_len, kv_heads, group_size, HD
        )
        key_block = lax.dynamic_index_in_dim(passage_keys, source, 0, keepdims=False).reshape(
            length, kv_heads, HD
        )
        value_block = lax.dynamic_index_in_dim(passage_values, source, 0, keepdims=False).reshape(
            length, kv_heads, HD
        )
        pick_rows = lax.dynamic_index_in_dim(all_picks, request, 0, keepdims=False)
        pick_list = lax.dynamic_index_in_dim(pick_rows, slot_cite[slot_index], 0, keepdims=False)
        dropped = jnp.any(pick_list[:, None] == positions[None, :], axis=0)
        scores = (
            jnp.einsum("skgd,lkd->skgl", query_block, key_block, preferred_element_type=jnp.float32)
            * score_scale
        )
        scores = jnp.where(dropped, very_low, scores)
        slot_max = jnp.max(scores, axis=-1)
        weights = jnp.exp(scores - slot_max[..., None])
        slot_sum = jnp.where(active, jnp.sum(weights, axis=-1), 0.0).reshape(suffix_len, head_count)
        slot_acc = jnp.einsum(
            "skgl,lkd->skgd",
            weights.astype(jnp.bfloat16),
            value_block,
            preferred_element_type=jnp.float32,
        )
        slot_acc = jnp.where(active, slot_acc, 0.0).reshape(suffix_len, head_count, HD)
        slot_max = jnp.where(active, slot_max, very_low).reshape(suffix_len, head_count)
        old_max = lax.dynamic_index_in_dim(row_max, request, 0, keepdims=False)
        old_sum = lax.dynamic_index_in_dim(row_sum, request, 0, keepdims=False)
        old_acc = lax.dynamic_index_in_dim(row_acc, request, 0, keepdims=False).reshape(
            suffix_len, head_count, HD
        )
        new_max = jnp.maximum(old_max, slot_max)
        old_factor = jnp.exp(old_max - new_max)
        new_factor = jnp.exp(slot_max - new_max)
        new_sum = old_sum * old_factor + slot_sum * new_factor
        new_acc = (old_acc * old_factor[..., None] + slot_acc * new_factor[..., None]).reshape(
            suffix_len, row_width
        )
        row_max = lax.dynamic_update_index_in_dim(row_max, new_max, request, 0)
        row_sum = lax.dynamic_update_index_in_dim(row_sum, new_sum, request, 0)
        row_acc = lax.dynamic_update_index_in_dim(row_acc, new_acc, request, 0)
        return (row_max, row_sum, row_acc)

    def slot_step(slot_index, loop_state):
        return attend_slot(slot_index, loop_state)

    start_state = (
        jnp.full((total_requests, suffix_len, head_count), very_low, jnp.float32),
        jnp.zeros((total_requests, suffix_len, head_count), jnp.float32),
        jnp.zeros((total_requests, suffix_len, row_width), jnp.float32),
    )
    row_max, row_sum, row_acc = lax.fori_loop(0, local_passages * PMOST, slot_step, start_state)
    partial_value = (
        row_acc.reshape(total_requests, suffix_len, head_count, HD)
        / jnp.maximum(row_sum, 1.0)[..., None]
    ).astype(jnp.bfloat16)
    ceiling_all = lax.pmax(row_max.astype(jnp.bfloat16), "pass").astype(row_max.dtype)
    weight_share = row_sum * jnp.exp(row_max - ceiling_all)
    weighted = lax.optimization_barrier(partial_value).astype(jnp.float32) * weight_share[..., None]
    far_sum, far_weight = (
        lax.psum_scatter(
            weighted.reshape(total_requests, suffix_len, row_width),
            "pass",
            scatter_dimension=0,
            tiled=True,
        ),
        lax.psum_scatter(weight_share, "pass", scatter_dimension=0, tiled=True),
    )
    own_ceiling = lax.dynamic_slice_in_dim(
        ceiling_all, my_place * local_requests, local_requests, 0
    )
    ceiling = jnp.maximum(host_max, own_ceiling)
    near_scale = jnp.exp(host_max - ceiling)
    far_scale = jnp.exp(own_ceiling - ceiling)
    numerator = (
        host_acc * near_scale[..., None]
        + far_sum.reshape(local_requests, suffix_len, head_count, HD) * far_scale[..., None]
    )
    denominator = host_sum * near_scale + far_weight * far_scale
    attended = (
        (numerator / denominator[..., None])
        .reshape(local_requests, suffix_len, row_width)
        .astype(jnp.bfloat16)
    )
    return lax.all_to_all(attended, "kv", split_axis=1, concat_axis=2, tiled=True)


def solution(mesh):
    placed = (
        P("pass", None, "kv"),
        P("pass", None, "kv"),
        P("pass", None, "kv"),
        P("pass", None, "kv"),
        P("pass", None, "kv"),
        P("pass", None, None, "kv"),
        P("pass", None, None, "kv"),
        P("pass", None),
        P("pass", None, None),
    )
    return jax.shard_map(
        body, mesh=mesh, in_specs=placed, out_specs=P("pass", "kv", None), check_vma=False
    )
```

profile of v0, /device:TPU:0, one launch (start us, length us, event | category | flops | bytes accessed | tf_op | source)
XLA Modules:
  0.0 384.9 jit_solution(8592516703680501009)
XLA Ops:
  7.3 10.3 %all-gather = s32[8,1,8]{2,1,0:T(1,128)S(1)} all-gather(s32[1,1,8]{2,1,0:T(1,128)} %bitcast.228), channel_id=1, replica_groups=mesh['pass'=8,'kv'=4] {'pass'}, dimensions={0}, use_global_device_ids=true | all-gather | bytes 288 | tf_op jit(solution)/shard_map/all_gather | solution.py:36
  18.9 8.9 %all_gather.10 = s32[8,8,128]{2,1,0:T(8,128)S(1)} all-gather(s32[1,8,128]{2,1,0:T(8,128)} %param.19), channel_id=1, replica_groups=mesh['pass'=8,'kv'=4] {'pass'}, dimensions={0}, use_global_device_ids=true | all-gather | bytes 36864 | tf_op jit(solution)/shard_map/all_gather | solution.py:37
  27.8 7.7 %all-gather.3.cloned.1.call-done = bf16[8,64,1024]{2,1,0:T(8,128)(2,1)} async-done(((bf16[1,64,1024]{2,1,0:T(8,128)(2,1)}), bf16[8,64,1024]{2,1,0:T(8,128)(2,1)}) %all-gather.3.cloned.1.call-update) | async-done | bytes 1048592 | tf_op jit(solution)/shard_map/all_gather | solution.py:39
  35.8 255.6 %while.21 = (s32[]{:T(128)}, f32[8,64,8]{1,2,0:T(8,128)S(1)}, f32[8,64,8]{1,2,0:T(8,128)S(1)}, f32[8,64,1024]{2,0,1:T(8,128)S(1)}, s32[16]{0:T(128)S(1)}, /*inde...) while((s32[]{:T(128)}, f32[8,64,8]{1,2,0:T(8,128)S(1)}, ...), condition=%wide.region_12.13_spmd.clone, body=%wide.region_8.12_spmd.clone.sunk | while | flops 274731008 | bytes 10676685 | solution.py:154
  46.6 2.2 fusion.84
  50.1 1.7 dynamic_update_slice.43
  62.6 2.2 fusion.84
  66.1 1.7 dynamic_update_slice.43
  74.4 1.5 bitcast_reduce_fusion.3
  78.5 2.2 fusion.84
  82.1 1.7 dynamic_update_slice.43
  94.5 2.2 fusion.84
  98.0 1.7 dynamic_update_slice.43
  106.4 1.5 bitcast_reduce_fusion.3
  110.5 2.2 fusion.84
  114.0 1.7 dynamic_update_slice.43
  126.5 2.2 fusion.84
  130.0 1.7 dynamic_update_slice.43
  142.4 2.2 fusion.84
  145.9 1.7 dynamic_update_slice.43
  158.4 2.2 fusion.84
  161.9 1.7 dynamic_update_slice.43
  170.3 1.5 bitcast_reduce_fusion.3
  174.4 2.2 fusion.84
  177.9 1.7 dynamic_update_slice.43
  190.4 2.2 fusion.84
  193.9 1.7 dynamic_update_slice.43
  202.2 1.5 bitcast_reduce_fusion.3
  206.3 2.2 fusion.84
  209.8 1.7 dynamic_update_slice.43
  222.3 2.2 fusion.84
  225.8 1.7 dynamic_update_slice.43
  238.3 2.2 fusion.84
  241.8 1.7 dynamic_update_slice.43
  254.3 2.2 fusion.84
  257.8 1.7 dynamic_update_slice.43
  270.2 2.2 fusion.84
  273.7 1.7 dynamic_update_slice.43
  286.2 2.2 fusion.84
  289.7 1.7 dynamic_update_slice.43
  291.4 23.5 %pmax.7 = bf16[8,64,8]{1,2,0:T(8,128)(2,1)S(1)} all-reduce(bf16[8,64,8]{1,2,0:T(8,128)(2,1)S(1)} %convert_element_type.44), channel_id=1, replica_groups=mesh['pass'=8,'kv'=4] {'pass'}, use_global_device_ids=true, to_apply=%region_13.14 | all-reduce | flops 4096 | bytes 16384 | tf_op jit(solution)/shard_map/pmax | solution.py:159
  315.8 1.6 fusion.31
  318.3 1.6 convert_multiply_fusion
  319.8 1.5 reshape.426
  323.7 22.4 %all-reduce = f32[8,64,8]{1,2,0:T(8,128)S(1)} all-reduce(f32[8,64,8]{1,2,0:T(8,128)S(1)} %get-tuple-element.393), channel_id=3, replica_groups=mesh['pass'=8,'kv'=4] {'pass'}, use_global_device_ids=true, to_apply=%region_17.18.clone | all-reduce | flops 4096 | bytes 32768
  348.6 14.2 %reduce-scatter.2.cloned.1.call-done = f32[1,64,1024]{2,1,0:T(8,128)} async-done(((f32[8,64,1024]{2,1,0:T(8,128)}), f32[1,64,1024]{2,1,0:T(8,128)}) %reduce-scatter.2.cloned.1.call-update) | async-done | bytes 262160 | tf_op jit(solution)/shard_map/reduce_scatter | solution.py:163
  363.2 1.6 fusion.67
  366.8 10.5 %all_to_all.18 = bf16[4,2,8192]{2,1,0:T(2,128)(2,1)S(1)} all-to-all(bf16[4,2,8192]{2,1,0:T(2,128)(2,1)S(1)} %reshape.441), channel_id=1, replica_groups=mesh['pass'=8,'kv'=4] {'kv'}, dimensions={0} | all-to-all | bytes 262144 | tf_op jit(solution)/shard_map/all_to_all | solution.py:187
  (327 shorter events, 130.3 us)
Async XLA Ops:
  6.5 316.7 %copy-start = (bf16[1,8,128,128]{3,2,1,0:T(8,128)(2,1)S(1)}, bf16[1,8,128,128]{3,2,1,0:T(8,128)(2,1)}, u32[]{:S(2)}) copy-start(bf16[1,8,128,128]{3,2,1,0:T(8,128)(2,1)} %param.16) | copy-start | bytes 786436
  6.5 29.0 %all-gather.3.cloned.1.call-start = ((), (), s32[]{:S(2)}) async-start(), calls=%async_computation.2 | async-start | bytes 1179648 | tf_op jit(solution)/shard_map/all_gather | solution.py:39
  7.3 355.5 %reduce-scatter.2.cloned.1.call-start = ((), (), s32[]{:S(2)}) async-start(), calls=%async_computation.3 | async-start | bytes 2359296 | tf_op jit(solution)/shard_map/reduce_scatter | solution.py:163
  321.4 0.9 copy-start.1
  321.4 0.9 copy-start.5
  321.4 1.5 copy-start.3
  323.2 24.4 %copy-start.2 = (bf16[1,8,128,128]{3,2,1,0:T(8,128)(2,1)S(1)}, bf16[1,8,128,128]{3,2,1,0:T(8,128)(2,1)}, u32[]{:S(2)}) copy-start(bf16[1,8,128,128]{3,2,1,0:T(8,128)(2,1)} %param.17) | copy-start | bytes 786436
  346.2 1.9 copy-start.4
Sparse Core Ops, SparseCore 0:
  9.2 26.2 all-gather.2
  321.5 41.2 reduce-scatter.1
where the time goes:
time: 388 us; the launch traced here: 385 us
  local copies, waits for them, and re-layouts  90.6 us (23%)
  blocking collectives  75.6 us (19%)
  loops' own time  68.5 us (18%)
  matrix products  60.9 us (16%)
  other arithmetic  52.9 us (14%)
  waiting for transfers between devices  22.6 us (6%)
  between operations  13.7 us (4%)
    another operation x1, loops' own time, body(): lax.fori_loop(0, local_passages * PMOST, slot_step, start_state)  68.5 us
    dot_general x16, matrix products, attend_slot(): jnp.einsum('skgl,lkd->skgd', weights.astype(jnp.bfloat16), value_block, p...  35.8 us
    dynamic_update_slice x16, local copies, waits for them, and re-layouts, attend_slot(): row_acc = lax.dynamic_update_index_in_dim(row_acc, new_acc, request, 0)  26.8 us
    dot_general x16, matrix products, attend_slot(): jnp.einsum('skgd,lkd->skgl', query_block, key_block, preferred_element_ty...  23.6 us
    pmax x1, blocking collectives, body(): lax.pmax(row_max.astype(jnp.bfloat16), 'pass').astype(row_max.dtype)  23.5 us
    unnamed x1, blocking collectives  22.4 us
    while x32, local copies, waits for them, and re-layouts  15 us
    reduce_scatter x1, waiting for transfers between devices, body(): lax.psum_scatter(weighted.reshape(total_requests, suffix_len, row_width),...  14.2 us
  transfers between devices with their start and end apart: 2, of which 2 were waited for; matrix products, arithmetic and copies ran while one was open for 1% of the time, Pallas kernels for 0%

commit v1 on v0

v1 whole, which is shorter than its diff:
```python
import functools
import math

import jax
import jax.numpy as jnp
from jax import lax
from jax.experimental import pallas as pl
from jax.experimental.pallas import tpu as pltpu
from jax.sharding import PartitionSpec as P

HD = 128
MESH = pl.DeviceIdType.MESH
very_low = -1e30
FACTOR = math.log2(math.e) / math.sqrt(HD)
ONES = 16
PMOST = 4
HALVES = 2
CHUNK = 256
KEYS = 256


def nt_dot(a, b):
    return lax.dot_general(a, b, (((1,), (1,)), ((), ())), preferred_element_type=jnp.float32)


def nn_dot(a, b):
    return jnp.dot(a, b, preferred_element_type=jnp.float32)


def stack_heads(rows, group_size):
    return jnp.concatenate([rows[:, g * HD : (g + 1) * HD] for g in range(group_size)], axis=0)


def fused_kernel(
    n,
    kv,
    q_ref,
    sk_ref,
    sv_ref,
    fk_ref,
    fv_ref,
    k_hbm,
    v_hbm,
    cite_ref,
    sel_ref,
    result,
    cite_buf,
    cite_in,
    sk_buf,
    sv_buf,
    fk_buf,
    fv_buf,
    k_ref,
    v_ref,
    v_t,
    q_low,
    q_high,
    cite_all,
    sel_all,
    bias,
    first,
    second,
    peak,
    slot_acc,
    slot_top,
    host_acc,
    host_max,
    mine_acc,
    mine_stat,
    away_out,
    away_stat,
    pair_out,
    pair_stat,
    send_out,
    send_stat,
    got_out,
    got_stat,
    kv_send,
    kv_recv,
    cites,
    slot_request,
    slot_cite,
    pair_slot,
    pair_live,
    in_sem,
    own_sem,
    gather_send,
    gather_recv,
    near_send,
    near_recv,
    pair_send_sem,
    pair_recv_sem,
    send_sem,
    recv_sem,
    kv_send_sem,
    kv_recv_sem,
):
    q_all = (q_low, q_high)
    me = lax.axis_index("pass")
    my_kv = lax.axis_index("kv")
    chip, core = me // 2, me % 2
    chips = n // 2
    sibling = chip * 2 + (1 - core)
    tokens = q_ref.shape[1]
    group_size = q_ref.shape[2] // HD
    heads = group_size // HALVES
    lanes = heads * tokens
    cut = heads * HD
    part = tokens // kv
    local, length, _ = k_ref.shape
    cite_count, picks = sel_all.shape[1:]
    slots = local * PMOST

    def target_chip(off):
        return (chip + off) % chips

    def origin(off, lane):
        return ((chip + chips - off) % chips) * 2 + lane

    loads = [
        pltpu.make_async_copy(source, place, in_sem.at[i])
        for i, (source, place) in enumerate(
            (
                (cite_ref, cite_in),
                (v_hbm, v_ref),
                (fk_ref, fk_buf),
                (fv_ref, fv_buf),
                (sk_ref, sk_buf),
                (sv_ref, sv_buf),
                (k_hbm, k_ref),
            )
        )
    ]
    for copy in loads:
        copy.start()

    sources = [cite_buf, sel_ref.at[0]] + [
        q_ref.at[0, :, h * cut : (h + 1) * cut] for h in range(HALVES)
    ]

    def place_of(i, slot):
        if i == 0:
            return cite_all.at[slot]
        if i == 1:
            return sel_all.at[slot]
        return q_all[i - 2].at[slot]

    own = [pltpu.make_async_copy(sources[i], place_of(i, me), own_sem.at[i]) for i in range(4)]
    for i in (2, 3, 1):
        own[i].start()
    barrier = pltpu.get_barrier_semaphore()
    for other in [sibling] + [target_chip(off) * 2 + core for off in range(1, chips)]:
        pl.semaphore_signal(barrier, inc=1, device_id={"pass": other}, device_id_type=MESH)
    for off in range(1, kv):
        pl.semaphore_signal(
            barrier, inc=1, device_id={"kv": (my_kv + off) % kv}, device_id_type=MESH
        )
    cite_buf[...] = jnp.zeros_like(cite_buf)
    loads[0].wait()
    cite_buf[0:1, 0:cite_count] = cite_in[...]
    own[0].start()
    pl.semaphore_wait(barrier, chips + kv - 1)

    def far(i, off, slot):
        return pltpu.make_async_remote_copy(
            src_ref=sources[i],
            dst_ref=place_of(i, slot),
            send_sem=gather_send.at[i, off],
            recv_sem=gather_recv.at[i, off],
            device_id={"pass": target_chip(off) * 2 + core},
            device_id_type=MESH,
        )

    def near(i, off, slot):
        return pltpu.make_async_remote_copy(
            src_ref=sources[i] if off == 0 else place_of(i, slot),
            dst_ref=place_of(i, slot),
            send_sem=near_send.at[i, off],
            recv_sem=near_recv.at[i, off],
            device_id={"pass": sibling},
            device_id_type=MESH,
        )

    sends = []

    def launch(copy):
        copy.start()
        sends.append(copy)

    for i in range(4):
        for off in range(1, chips):
            launch(far(i, off, me))
        launch(near(i, 0, me))

    def pass_on(i):
        for off in range(1, chips):
            slot = origin(off, core)
            far(i, off, slot).wait_recv()
            launch(near(i, off, slot))

    def settle(i):
        for off in range(chips):
            near(i, off, origin(off, 1 - core)).wait_recv()

    loads[1].wait()
    for p in range(local):
        v_t[p, 0:HD, :] = v_ref[p].T
        v_t[p, HD:, :] = jnp.ones((ONES, length), jnp.bfloat16)
    pass_on(0)
    pass_on(1)

    for copy in loads[2:]:
        copy.wait()
    for copy in own:
        copy.wait()
    fresh = fk_ref.shape[1] * fk_ref.shape[2]
    fk = fk_buf[0].reshape(fresh, HD)
    fv_t = fv_buf[0].reshape(fresh, HD).T
    fv_t = jnp.concatenate([fv_t, jnp.ones((ONES, fresh), jnp.bfloat16)], axis=0)
    sv_t = sv_buf[0].astype(jnp.float32).T.astype(jnp.bfloat16)
    sv_t = jnp.concatenate([sv_t, jnp.ones((ONES, tokens), jnp.bfloat16)], axis=0)
    for h in range(HALVES):
        block = stack_heads(q_all[h][me], heads)
        fs = nt_dot(fk, block)
        ss = nt_dot(sk_buf[0], block)
        key_at = lax.broadcasted_iota(jnp.int32, (tokens, lanes), 0)
        token_at = lax.broadcasted_iota(jnp.int32, (tokens, lanes), 1) % tokens
        ss = jnp.where(key_at <= token_at, ss, very_low)
        top = jnp.maximum(
            jnp.max(fs, axis=0, keepdims=True), jnp.max(ss, axis=0, keepdims=True)
        )
        fw = jnp.exp2((fs - top) * FACTOR).astype(jnp.bfloat16)
        sw = jnp.exp2((ss - top) * FACTOR).astype(jnp.bfloat16)
        host_acc[h] = nn_dot(fv_t, fw) + nn_dot(sv_t, sw)
        host_max[h] = jnp.broadcast_to(top, (8, lanes))

    settle(0)
    settle(1)
    to_scalar = pltpu.make_async_copy(cite_all, cites, in_sem.at[0])
    to_scalar.start()
    pass_on(2)
    to_scalar.wait()
    for i in range(slots):
        slot_request[i] = 0
        slot_cite[i] = 0

    def tabulate(r, counts):
        names = [cites[r, 0, c] for c in range(cite_count)]
        after = []
        for p in range(local):
            name = me * local + p
            hit, at = jnp.int32(0), jnp.int32(0)
            for c in range(cite_count):
                same = (names[c] == name).astype(jnp.int32)
                hit = jnp.maximum(hit, same)
                at = jnp.maximum(at, same * c)
            rank = counts[p]
            pair_live[r * local + p] = hit
            pair_slot[r * local + p] = p * PMOST + jnp.minimum(rank, PMOST - 1)
            for k in range(PMOST):
                here = hit * (rank == k).astype(jnp.int32)
                i = p * PMOST + k
                slot_request[i] = slot_request[i] + here * r
                slot_cite[i] = slot_cite[i] + here * at
            after.append(rank + hit)
        return tuple(after)

    lax.fori_loop(0, n, tabulate, (jnp.int32(0),) * local)

    def fill_bias(i, carry):
        at = lax.broadcasted_iota(jnp.int32, (length, picks), 0)
        picked = sel_all[slot_request[i], pl.ds(slot_cite[i], 1), :]
        bias[i] = jnp.where(at == picked, very_low, 0.0).astype(jnp.bfloat16)
        return carry

    lax.fori_loop(0, slots, fill_bias, 0)
    settle(2)

    steps = [slice(lo, lo + KEYS) for lo in range(0, length, KEYS)]

    def score_steps(h, i, place, side):
        p = i // PMOST
        q = stack_heads(q_all[h][slot_request[i]], heads)
        q = jnp.concatenate([q, jnp.ones((lanes, picks), jnp.bfloat16)], axis=1)
        highest = None
        for at in steps:
            keys = jnp.concatenate([k_ref[p, at, :], bias[i, at, :]], axis=1)
            s = nt_dot(keys, q)
            place[at, :] = s
            here = jnp.max(s.reshape(KEYS // 8, 8, lanes), axis=0)
            highest = here if highest is None else jnp.maximum(highest, here)
            yield
        peak[side] = jnp.broadcast_to(jnp.max(highest, axis=0, keepdims=True), (8, lanes))

    def weigh_steps(i, place, side):
        p = i // PMOST
        top = peak[side]
        slot_top[i] = top
        added = None
        for at in steps:
            w = jnp.exp2((place[at, :] - top[0:1]) * FACTOR).astype(jnp.bfloat16)
            here = nn_dot(v_t[p, :, at], w)
            added = here if added is None else added + here
            yield
        slot_acc[i] = added

    def together(*parts):
        waiting = list(parts)
        while waiting:
            waiting = [part for part in waiting if next(part, True) is None]

    def two_slots(h):
        def step(t, carry):
            i = 2 * t
            together(weigh_steps(i, first, 0), score_steps(h, i + 1, second, 1))
            later = jnp.minimum(i + 2, slots - 1)
            together(weigh_steps(i + 1, second, 1), score_steps(h, later, first, 0))
            return carry

        return step

    def flash_merge(outs, stats):
        ceiling = stats[0][0]
        for top, _ in stats[1:]:
            ceiling = jnp.maximum(ceiling, top)
        numer, denom = 0.0, 0.0
        for out, (top, weight) in zip(outs, stats):
            scale = jnp.exp2((top - ceiling) * FACTOR)
            if out.dtype == jnp.bfloat16:
                scale = weight * scale
                numer = numer + out.astype(jnp.float32) * scale
                denom = denom + scale
            else:
                numer = numer + out * scale
                denom = denom + weight * scale
        return ceiling, numer, denom

    def of_request(r):
        outs, stats = [], []
        for p in range(local):
            i, live = pair_slot[r * local + p], pair_live[r * local + p].astype(jnp.float32)
            block = slot_acc[i]
            top = slot_top[i][0:1] * live + very_low * (1.0 - live)
            outs.append(block[0:HD] * live)
            stats.append((top, block[HD : HD + 1] * live))
        return flash_merge(outs, stats)

    def stat_block(top, denom):
        return jnp.concatenate(
            [jnp.broadcast_to(top, (4, lanes)), jnp.broadcast_to(denom, (4, lanes))]
        )

    def stats_of(block):
        return block[0:1, :], block[4:5, :]

    def to_sibling(i, h, off):
        source, place = ((away_out, pair_out), (away_stat, pair_stat))[i]
        return pltpu.make_async_remote_copy(
            src_ref=source.at[off, h],
            dst_ref=place.at[off, h],
            send_sem=pair_send_sem.at[i, h, off],
            recv_sem=pair_recv_sem.at[i, h, off],
            device_id={"pass": sibling},
            device_id_type=MESH,
        )

    def to_chip(i, h, off):
        source, place = ((send_out, got_out), (send_stat, got_stat))[i]
        return pltpu.make_async_remote_copy(
            src_ref=source.at[off, h],
            dst_ref=place.at[off, h],
            send_sem=send_sem.at[i, h, off],
            recv_sem=recv_sem.at[i, h, off],
            device_id={"pass": target_chip(off) * 2 + core},
            device_id_type=MESH,
        )

    def across(h, off, target, slot):
        return pltpu.make_async_remote_copy(
            src_ref=kv_send.at[h, target],
            dst_ref=kv_recv.at[h, slot],
            send_sem=kv_send_sem.at[h, off],
            recv_sem=kv_recv_sem.at[h, off],
            device_id={"kv": target},
            device_id_type=MESH,
        )

    order = list(range(1, chips)) + [0]

    def collect(h):
        for off in order:
            top, numer, denom = of_request(target_chip(off) * 2 + 1 - core)
            away_out[off, h] = (numer * (1.0 / jnp.maximum(denom, 1.0))).astype(jnp.bfloat16)
            away_stat[off, h] = stat_block(top, denom)
            for i in (1, 0):
                launch(to_sibling(i, h, off))
        for off in order:
            top, numer, denom = of_request(target_chip(off) * 2 + core)
            mine_acc[off, h] = numer
            mine_stat[off, h] = stat_block(top, denom)

    def of_chip(h, off):
        for i in range(2):
            to_sibling(i, h, off).wait_recv()
        return (
            [mine_acc[off, h], pair_out[off, h]],
            [stats_of(mine_stat[off, h]), stats_of(pair_stat[off, h])],
        )

    def exchange(h):
        for off in range(1, chips):
            top, numer, denom = flash_merge(*of_chip(h, off))
            send_out[off, h] = (numer * (1.0 / jnp.maximum(denom, 1.0))).astype(jnp.bfloat16)
            send_stat[off, h] = stat_block(top, denom)
            for i in (1, 0):
                launch(to_chip(i, h, off))

    def finish(h):
        outs, stats = of_chip(h, 0)
        outs.append(host_acc[h, 0:HD])
        stats.append((host_max[h, 0:1], host_acc[h, HD : HD + 1]))
        for off in range(1, chips):
            for i in range(2):
                to_chip(i, h, off).wait_recv()
            outs.append(got_out[off, h])
            stats.append(stats_of(got_stat[off, h]))
        _, numer, denom = flash_merge(outs, stats)
        done = (numer / denom).T
        for j in range(kv):
            block = [done[g * tokens + j * part : g * tokens + (j + 1) * part] for g in range(heads)]
            kv_send[h, j] = jnp.concatenate(block, axis=1).astype(jnp.bfloat16)
        for off in range(1, kv):
            launch(across(h, off, (my_kv + off) % kv, my_kv))
        kv_recv[h, my_kv] = kv_send[h, my_kv]

    pairs, early = slots // 2, slots // 8
    together(score_steps(0, 0, first, 0))
    lax.fori_loop(0, early, two_slots(0), 0)
    pass_on(3)
    lax.fori_loop(early, pairs, two_slots(0), 0)
    collect(0)
    settle(3)
    together(score_steps(1, 0, first, 0))
    lax.fori_loop(0, early, two_slots(1), 0)
    exchange(0)
    lax.fori_loop(early, pairs, two_slots(1), 0)
    collect(1)
    exchange(1)
    finish(0)
    finish(1)
    for h in range(HALVES):
        for off in range(1, kv):
            across(h, off, (my_kv + off) % kv, (my_kv + kv - off) % kv).wait_recv()
        for i in range(kv):
            lo = (i * HALVES + h) * cut
            result[0, :, lo : lo + cut] = kv_recv[h, i]
    for copy in sends:
        copy.wait_send()


VM = pl.BlockSpec(memory_space=pltpu.VMEM)
ANY = pl.BlockSpec(memory_space=pl.ANY)
LIMIT = 62 * 1024 * 1024


def body(
    n,
    kv,
    queries,
    suffix_keys,
    suffix_values,
    passage_keys,
    passage_values,
    fresh_keys,
    fresh_values,
    citations,
    selected,
):
    _, tokens, width = queries.shape
    lanes = tokens * width // HD // HALVES
    local, length, _ = passage_keys.shape
    _, cite_count, picks = selected.shape
    chips = n // 2
    slots = local * PMOST
    bf, f32, i32 = jnp.bfloat16, jnp.float32, jnp.int32
    dma = pltpu.SemaphoreType.DMA
    tall = HD + ONES
    out_block = pltpu.VMEM((chips, HALVES, HD, lanes), bf)
    stat_block = pltpu.VMEM((chips, HALVES, 8, lanes), f32)
    kv_block = pltpu.VMEM((HALVES, kv, tokens // kv, width // HALVES), bf)
    return pl.pallas_call(
        functools.partial(fused_kernel, n, kv),
        out_shape=jax.ShapeDtypeStruct((1, tokens // kv, width * kv), bf),
        in_specs=[ANY] * 9,
        out_specs=VM,
        scratch_shapes=[
            pltpu.VMEM((8, 128), i32),
            pltpu.VMEM(citations.shape, i32),
            pltpu.VMEM(suffix_keys.shape, bf),
            pltpu.VMEM(suffix_values.shape, bf),
            pltpu.VMEM(fresh_keys.shape, bf),
            pltpu.VMEM(fresh_values.shape, bf),
            pltpu.VMEM(passage_keys.shape, bf),
            pltpu.VMEM(passage_values.shape, bf),
            pltpu.VMEM((local, tall, length), bf),
            pltpu.VMEM((n, tokens, width // HALVES), bf),
            pltpu.VMEM((n, tokens, width // HALVES), bf),
            pltpu.VMEM((n, 8, 128), i32),
            pltpu.VMEM((n, cite_count, picks), i32),
            pltpu.VMEM((slots, length, picks), bf),
            pltpu.VMEM((length, lanes), f32),
            pltpu.VMEM((length, lanes), f32),
            pltpu.VMEM((2, 8, lanes), f32),
            pltpu.VMEM((slots, tall, lanes), f32),
            pltpu.VMEM((slots, 8, lanes), f32),
            pltpu.VMEM((HALVES, tall, lanes), f32),
            pltpu.VMEM((HALVES, 8, lanes), f32),
            pltpu.VMEM((chips, HALVES, HD, lanes), f32),
            stat_block,
            *([out_block, stat_block] * 4),
            kv_block,
            kv_block,
            pltpu.SMEM((n, 8, 128), i32),
            pltpu.SMEM((slots,), i32),
            pltpu.SMEM((slots,), i32),
            pltpu.SMEM((n * local,), i32),
            pltpu.SMEM((n * local,), i32),
            dma((7,)),
            dma((4,)),
            *([dma((4, chips))] * 4),
            *([dma((2, HALVES, chips))] * 4),
            dma((HALVES, kv)),
            dma((HALVES, kv)),
        ],
        compiler_params=pltpu.CompilerParams(
            collective_id=0, has_side_effects=True, vmem_limit_bytes=LIMIT
        ),
        name="fused_attention",
    )(
        queries,
        suffix_keys,
        suffix_values,
        fresh_keys,
        fresh_values,
        passage_keys,
        passage_values,
        citations,
        selected,
    )


def solution(mesh):
    placed = (
        P("pass", None, "kv"),
        P("pass", None, "kv"),
        P("pass", None, "kv"),
        P("pass", None, "kv"),
        P("pass", None, "kv"),
        P("pass", None, None, "kv"),
        P("pass", None, None, "kv"),
        P("pass", None),
        P("pass", None, None),
    )
    return jax.shard_map(
        functools.partial(body, mesh.shape["pass"], mesh.shape["kv"]),
        mesh=mesh,
        in_specs=placed,
        out_specs=P("pass", "kv", None),
        check_vma=False,
    )
```

time: 388 us -> 42.4 us (0.11)
  local copies, waits for them, and re-layouts: 90.6 us -> 1.57 us
  blocking collectives: 75.6 us -> 0 us
  loops' own time: 68.5 us -> 0 us
  matrix products: 60.9 us -> 0 us
  other arithmetic: 52.9 us -> 0 us
  Pallas kernels: 0 us -> 40.6 us
  waiting for transfers between devices: 22.6 us -> 0 us
  between operations: 13.7 us -> 0.01 us
    another operation x1 -> x0, loops' own time: 68.5 us -> none  [body(): lax.fori_loop(0, local_passages * PMOST, slot_step, start_state)]
    dot_general x36 -> x0, matrix products: 60.9 us -> none  [the longest x16 35.8 us: attend_slot(): jnp.einsum('skgl,lkd->skgd', weights.astype(jnp.bfloat16), value_block, p...]
    pallas_call x0 -> x1, Pallas kernels: none -> 40.6 us  [body(): pl.pallas_call(functools.partial(fused_kernel, n, kv), out_shape=jax.Shap...]
    dynamic_slice x48 -> x0, local copies, waits for them, and re-layouts: 32 us -> none  [the longest x16 10.7 us: attend_slot(): active = slot_live[slot_index]]
    dynamic_update_slice x16 -> x0, local copies, waits for them, and re-layouts: 26.8 us -> none  [attend_slot(): row_acc = lax.dynamic_update_index_in_dim(row_acc, new_acc, request, 0)]
    pmax x1 -> x0, blocking collectives: 23.5 us -> none  [body(): lax.pmax(row_max.astype(jnp.bfloat16), 'pass').astype(row_max.dtype)]
    unnamed x1 -> x0, blocking collectives: 22.4 us -> none
    all_gather x2 -> x0, blocking collectives: 19.2 us -> none  [the longest x1 10.3 us: body(): lax.all_gather(citations, 'pass', axis=0, tiled=True)]
  transfers between devices with their start and end apart: 2 -> 0, of which waited for: 2 -> 0; matrix products, arithmetic and copies ran while one was open for 1% -> 0% of each run, Pallas kernels for 0% -> 0%
where the time goes in v1:
time: 42.4 us; the launch traced here: 42.2 us
  Pallas kernels  40.6 us (96%)
  local copies, waits for them, and re-layouts  1.57 us (4%)
    pallas_call x1, Pallas kernels, body(): pl.pallas_call(functools.partial(fused_kernel, n, kv), out_shape=jax.Shap...  40.6 us
    unnamed x1, local copies, waits for them, and re-layouts  1.57 us

profile of v1, /device:TPU:0, one launch (start us, length us, event | category | flops | bytes accessed | tf_op | source)
XLA Modules:
  0.0 42.2 jit_solution(1947605653921677963)
XLA Ops:
  0.0 40.6 %fused_attention.1 = bf16[1,16,4096]{2,1,0:T(8,128)(2,1)} custom-call(bf16[1,64,1024]{2,1,0:T(8,128)(2,1)} %q_ref.1, bf16[1,64,128]{2,1,0:T(8,128)(2,1)} %sk_ref.1, bf16[1,64,128]{2,1,0:T(8,128)(2,1)} %sv_ref.1, bf16[1,8,128,128]{3,2,1,0:T(8,128)(2,1)} %fk_ref.1, bf16[1,8,128,128]{3,2,1,0:T(8,128)(2,1)} %fv_ref.1, bf16[4,1024,128]{2,1,0:T(8,128)(2,1)} %k_hbm.1, ...), custom_call_target="tpu_custom_call" | custom-call | tf_op jit(solution)/shard_map/fused_attention/pallas_call | solution.py:491
  40.6 1.6 %copy.11 = bf16[1,16,4096]{2,1,0:T(8,128)(2,1)} copy(bf16[1,16,4096]{2,1,0:T(8,128)(2,1)} %fused_attention.1) | data formatting | bytes 262144

commit v2 on v1

--- a/solution.py
+++ b/solution.py
@@ -213,32 +213,10 @@
         copy.wait()
     for copy in own:
         copy.wait()
-    fresh = fk_ref.shape[1] * fk_ref.shape[2]
-    fk = fk_buf[0].reshape(fresh, HD)
-    fv_t = fv_buf[0].reshape(fresh, HD).T
-    fv_t = jnp.concatenate([fv_t, jnp.ones((ONES, fresh), jnp.bfloat16)], axis=0)
-    sv_t = sv_buf[0].astype(jnp.float32).T.astype(jnp.bfloat16)
-    sv_t = jnp.concatenate([sv_t, jnp.ones((ONES, tokens), jnp.bfloat16)], axis=0)
-    for h in range(HALVES):
-        block = stack_heads(q_all[h][me], heads)
-        fs = nt_dot(fk, block)
-        ss = nt_dot(sk_buf[0], block)
-        key_at = lax.broadcasted_iota(jnp.int32, (tokens, lanes), 0)
-        token_at = lax.broadcasted_iota(jnp.int32, (tokens, lanes), 1) % tokens
-        ss = jnp.where(key_at <= token_at, ss, very_low)
-        top = jnp.maximum(
-            jnp.max(fs, axis=0, keepdims=True), jnp.max(ss, axis=0, keepdims=True)
-        )
-        fw = jnp.exp2((fs - top) * FACTOR).astype(jnp.bfloat16)
-        sw = jnp.exp2((ss - top) * FACTOR).astype(jnp.bfloat16)
-        host_acc[h] = nn_dot(fv_t, fw) + nn_dot(sv_t, sw)
-        host_max[h] = jnp.broadcast_to(top, (8, lanes))
-
     settle(0)
     settle(1)
     to_scalar = pltpu.make_async_copy(cite_all, cites, in_sem.at[0])
     to_scalar.start()
-    pass_on(2)
     to_scalar.wait()
     for i in range(slots):
         slot_request[i] = 0
@@ -266,6 +244,7 @@
         return tuple(after)
 
     lax.fori_loop(0, n, tabulate, (jnp.int32(0),) * local)
+    pass_on(2)
 
     def fill_bias(i, carry):
         at = lax.broadcasted_iota(jnp.int32, (length, picks), 0)
@@ -433,6 +412,21 @@
             launch(across(h, off, (my_kv + off) % kv, my_kv))
         kv_recv[h, my_kv] = kv_send[h, my_kv]
 
+    def attend_host(h):
+        block = stack_heads(q_all[h][me], heads)
+        fs = nt_dot(fk, block)
+        ss = nt_dot(sk_buf[0], block)
+        key_at = lax.broadcasted_iota(jnp.int32, (tokens, lanes), 0)
+        token_at = lax.broadcasted_iota(jnp.int32, (tokens, lanes), 1) % tokens
+        ss = jnp.where(key_at <= token_at, ss, very_low)
+        top = jnp.maximum(
+            jnp.max(fs, axis=0, keepdims=True), jnp.max(ss, axis=0, keepdims=True)
+        )
+        fw = jnp.exp2((fs - top) * FACTOR).astype(jnp.bfloat16)
+        sw = jnp.exp2((ss - top) * FACTOR).astype(jnp.bfloat16)
+        host_acc[h] = nn_dot(fv_t, fw) + nn_dot(sv_t, sw)
+        host_max[h] = jnp.broadcast_to(top, (8, lanes))
+
     pairs, early = slots // 2, slots // 8
     together(score_steps(0, 0, first, 0))
     lax.fori_loop(0, early, two_slots(0), 0)
@@ -446,8 +440,15 @@
     lax.fori_loop(early, pairs, two_slots(1), 0)
     collect(1)
     exchange(1)
-    finish(0)
-    finish(1)
+    fresh = fk_ref.shape[1] * fk_ref.shape[2]
+    fk = fk_buf[0].reshape(fresh, HD)
+    fv_t = fv_buf[0].reshape(fresh, HD).T
+    fv_t = jnp.concatenate([fv_t, jnp.ones((ONES, fresh), jnp.bfloat16)], axis=0)
+    sv_t = sv_buf[0].astype(jnp.float32).T.astype(jnp.bfloat16)
+    sv_t = jnp.concatenate([sv_t, jnp.ones((ONES, tokens), jnp.bfloat16)], axis=0)
+    for h in range(HALVES):
+        attend_host(h)
+        finish(h)
     for h in range(HALVES):
         for off in range(1, kv):
             across(h, off, (my_kv + off) % kv, (my_kv + kv - off) % kv).wait_recv()

time: 42.4 us -> 41.8 us (0.986)
  Pallas kernels: 40.6 us -> 40.1 us
    pallas_call x1, Pallas kernels: 40.6 us -> 40.1 us  [body(): pl.pallas_call(functools.partial(fused_kernel, n, kv), out_shape=jax.Shap...]
where the time goes in v2:
time: 41.8 us; the launch traced here: 41.6 us
  Pallas kernels  40.1 us (96%)
  local copies, waits for them, and re-layouts  1.57 us (4%)
    pallas_call x1, Pallas kernels, body(): pl.pallas_call(functools.partial(fused_kernel, n, kv), out_shape=jax.Shap...  40.1 us
    unnamed x1, local copies, waits for them, and re-layouts  1.57 us

profile of v2, /device:TPU:0, one launch (start us, length us, event | category | flops | bytes accessed | tf_op | source)
XLA Modules:
  0.0 41.6 jit_solution(17278574488218391743)
XLA Ops:
  0.0 40.1 %fused_attention.1 = bf16[1,16,4096]{2,1,0:T(8,128)(2,1)} custom-call(bf16[1,64,1024]{2,1,0:T(8,128)(2,1)} %q_ref.1, bf16[1,64,128]{2,1,0:T(8,128)(2,1)} %sk_ref.1, bf16[1,64,128]{2,1,0:T(8,128)(2,1)} %sv_ref.1, bf16[1,8,128,128]{3,2,1,0:T(8,128)(2,1)} %fk_ref.1, bf16[1,8,128,128]{3,2,1,0:T(8,128)(2,1)} %fv_ref.1, bf16[4,1024,128]{2,1,0:T(8,128)(2,1)} %k_hbm.1, ...), custom_call_target="tpu_custom_call" | custom-call | tf_op jit(solution)/shard_map/fused_attention/pallas_call | solution.py:492
  40.1 1.6 %copy.11 = bf16[1,16,4096]{2,1,0:T(8,128)(2,1)} copy(bf16[1,16,4096]{2,1,0:T(8,128)(2,1)} %fused_attention.1) | data formatting | bytes 262144

commit v3 on v2

--- a/solution.py
+++ b/solution.py
@@ -16,7 +16,7 @@
 PMOST = 4
 HALVES = 2
 CHUNK = 256
-KEYS = 256
+KEYS = 512
 
 
 def nt_dot(a, b):

time: 41.8 us -> 41.4 us (level)
  no operation moved by 1% of the time
where the time goes in v3:
time: 41.4 us; the launch traced here: 41.3 us
  Pallas kernels  39.7 us (96%)
  local copies, waits for them, and re-layouts  1.57 us (4%)
    pallas_call x1, Pallas kernels, body(): pl.pallas_call(functools.partial(fused_kernel, n, kv), out_shape=jax.Shap...  39.7 us
    unnamed x1, local copies, waits for them, and re-layouts  1.57 us

profile of v3, /device:TPU:0, one launch (start us, length us, event | category | flops | bytes accessed | tf_op | source)
XLA Modules:
  0.0 41.3 jit_solution(16823360784201895305)
XLA Ops:
  0.0 39.7 %fused_attention.1 = bf16[1,16,4096]{2,1,0:T(8,128)(2,1)} custom-call(bf16[1,64,1024]{2,1,0:T(8,128)(2,1)} %q_ref.1, bf16[1,64,128]{2,1,0:T(8,128)(2,1)} %sk_ref.1, bf16[1,64,128]{2,1,0:T(8,128)(2,1)} %sv_ref.1, bf16[1,8,128,128]{3,2,1,0:T(8,128)(2,1)} %fk_ref.1, bf16[1,8,128,128]{3,2,1,0:T(8,128)(2,1)} %fv_ref.1, bf16[4,1024,128]{2,1,0:T(8,128)(2,1)} %k_hbm.1, ...), custom_call_target="tpu_custom_call" | custom-call | tf_op jit(solution)/shard_map/fused_attention/pallas_call | solution.py:492
  39.7 1.6 %copy.11 = bf16[1,16,4096]{2,1,0:T(8,128)(2,1)} copy(bf16[1,16,4096]{2,1,0:T(8,128)(2,1)} %fused_attention.1) | data formatting | bytes 262144
